TPU v7x, 512 devices: a whole 4x8x8 slice. The times are simulated.
512 devices in a mesh: var: 8 (over y_hi, x), tm: 64 (over z, y_lo, core).
Axes of the slice: x: 4, y: 8 (y_hi: 2, y_lo: 4; y = y_hi * 4 + y_lo), z: 8, core: 2. Of those that a mesh axis runs over, the one named last changes fastest.
Arguments:
- frames: bfloat16 [32768, 1024], P('tm'), may hold values from -6 to 6
- span_start: int32 [8], P('var'), parts along dimension 0, may hold values from 0 to 30720
- span_length: int32 [8], P('var'), parts along dimension 0, may hold values from 512 to 2048
- ln_gain: float32 [1024], replicated, may hold values from 0.5 to 2
- w_in: bfloat16 [1024, 2048], P(None, 'tm'), may hold values from -0.1875 to 0.1875
- kernel: float32 [31, 1024], replicated, may hold values from -1 to 1
- bn_scale: float32 [1024], replicated, may hold values from 0.5 to 2
- bn_shift: float32 [1024], replicated, may hold values from -3 to 3
- w_out: bfloat16 [1024, 1024], P(None, 'tm'), may hold values from -0.1875 to 0.1875
Outputs:
- mixed: bfloat16 [262144, 1024], P(('var', 'tm')), parts along dimension 0
There are 8 independent parts, one for each index of `var`. A program takes and returns all parts, laid end to end along the dimension named above; an argument that names none is the same for every part. Nothing has to cross between parts.
Inputs may be any that keep to these rules, and one draw needn't show every extreme that they name: Occluded spans lie inside the sequence: span_start + span_length <= 32768.
All inputs are finite; a program needn't handle non-finite values.
Results may differ from a plain program's by a relative error of at most 0.005.
Values may be sent and summed in bfloat16 or wider, within the bound.
A program may use at most 64 MiB of HBM per device.

v0:
```python
import jax
import jax.numpy as jnp
from jax import lax
from jax.sharding import PartitionSpec as P


def padded_2(cells, sides, width):
    for axis, dim in sides:
        count = lax.axis_size(axis)
        ends = count - 1
        head = lax.slice_in_dim(cells, 0, width, axis=dim)
        tail = lax.slice_in_dim(cells, cells.shape[dim] - width, cells.shape[dim], axis=dim)
        cells = jnp.concatenate(
            [
                lax.ppermute(tail, axis, [(i, (i + 1) % count) for i in range(ends)]),
                cells,
                lax.ppermute(head, axis, [((i + 1) % count, i) for i in range(ends)]),
            ],
            axis=dim,
        )
    return cells


def normalize(masked, ln_gain):
    values = masked.astype(jnp.float32)
    average = jnp.mean(values, axis=1, keepdims=True)
    centred = values - average
    variance = jnp.mean(centred * centred, axis=1, keepdims=True)
    return (centred * lax.rsqrt(variance + 1e-05) * ln_gain).astype(jnp.bfloat16)


def shards(frames, span_start, span_length, ln_gain, w_in, kernel, bn_scale, bn_shift, w_out):
    frame_rows, channels = frames.shape
    reach = kernel.shape[0] // 2
    device_index = lax.axis_index("tm")
    position = device_index * frame_rows + lax.iota(jnp.int32, frame_rows)
    inside = (position >= span_start[0]) & (position < span_start[0] + span_length[0])
    masked = jnp.where(inside[:, None], jnp.zeros((), jnp.bfloat16), frames)
    normed = normalize(masked, ln_gain)
    full_in, full_out = (
        lax.all_gather(w_in, "tm", axis=1, tiled=True),
        lax.all_gather(w_out, "tm", axis=1, tiled=True),
    )
    lifted = jnp.dot(normed, full_in, preferred_element_type=jnp.float32)
    gated = (lifted[:, :channels] * jax.nn.sigmoid(lifted[:, channels:])).astype(jnp.bfloat16)
    padded = padded_2(gated, (("tm", 0),), reach).astype(jnp.float32)
    convolved = jnp.zeros((frame_rows, channels), jnp.float32)
    for offset in range(kernel.shape[0]):
        convolved = convolved + padded[offset : offset + frame_rows] * kernel[offset]
    activated = jax.nn.silu(convolved * bn_scale + bn_shift).astype(jnp.bfloat16)
    branch = jnp.dot(activated, full_out, preferred_element_type=jnp.float32)
    return (masked.astype(jnp.float32) + branch).astype(jnp.bfloat16)


def solution(mesh):
    return jax.shard_map(
        shards,
        mesh=mesh,
        in_specs=(
            P("tm", None),
            P("var"),
            P("var"),
            P(),
            P(None, "tm"),
            P(),
            P(),
            P(),
            P(None, "tm"),
        ),
        out_specs=P(("var", "tm"), None),
        check_vma=False,
    )
```

profile of v0, /device:TPU:1, one launch (start us, length us, event | category | flops | bytes accessed | tf_op | source)
XLA Modules:
  0.0 272.0 jit_solution(13192949939083735063)
XLA Ops:
  6.5 0.0 copy-start
  6.5 0.0 copy-start.1
  6.5 0.0 copy-start.2
  6.5 0.0 all-gather.3.cloned.1.call-start
  6.5 0.7 all-gather.3.cloned.1.call-update
  7.3 0.0 all-gather.5.cloned.1.call-start
  7.3 0.7 all-gather.5.cloned.1.call-update
  9.3 1.6 convert_reduce_fusion
  10.9 1.7 fusion.2
  12.7 0.0 copy-done.1
  12.7 0.1 fusion.53
  12.7 122.0 %all-gather.3.cloned.1.call-done = bf16[1024,2048]{0,1:T(8,128)(2,1)} async-done(((bf16[1024,32]{0,1:T(8,128)(2,1)}), bf16[1024,2048]{0,1:T(8,128)(2,1)}) %all-gather.3.cloned.1.call-update) | async-done | bytes 4194320 | tf_op jit(solution)/shard_map/all_gather | solution.py:41
  134.7 0.0 copy-done
  134.7 0.0 copy-done.2
  134.7 4.8 %fusion.43 = f32[512,2048]{1,0:T(8,128)S(1)} fusion(bf16[1024,2048]{0,1:T(8,128)(2,1)} %all-gather.3.cloned.1.call-done, f32[1024]{0:T(1024)S(1)} %copy-done.2, f32[512]{0:T(512)S(1)} %add_rsqrt_fusion, f32[512]{0:T(512)S(1)} %broadcast_multiply_fusion, bf16[512,1024]{1,0:T(8,128)(2,1)S(1)} %copy-done, pred[512]{0:T(512)(128)(4,1)S(1)} %fusion.50), kind=kOutput, calls=%fused_computation.80 | convolution fusion | flops 2150629376 | bytes 9445888 | tf_op jit(solution)/shard_map/dot_general | solution.py:44
  139.5 0.6 fusion.42
  140.1 0.0 copy-start.3
  140.1 0.0 copy-start.4
  140.2 3.2 %collective-permute-start = (bf16[15,1024]{1,0:T(8,128)(2,1)S(1)}, bf16[15,1024]{1,0:T(8,128)(2,1)S(1)}, u32[]{:S(2)}, u32[]{:S(2)}) collective-permute-start(bf16[15,1024]{1,0:T(8,128)(2,1)S(1)} %get-tuple-element.5), channel_id=1, source_target_pairs={{0,1},{1,2},{2,3},{3,4},{4,5},{5,6},{6,7},{7,8},{8,9},{9,10},{10,1... | collective-permute-start | bytes 92168 | tf_op jit(solution)/shard_map/ppermute | solution.py:15
  143.3 1.9 collective-permute-start.1
  145.3 0.0 collective-permute-done
  145.3 3.2 %collective-permute-done.1 = bf16[15,1024]{1,0:T(8,128)(2,1)S(1)} collective-permute-done((bf16[15,1024]{1,0:T(8,128)(2,1)S(1)}, bf16[15,1024]{1,0:T(8,128)(2,1)S(1)}, u32[]{:S(2)}, u32[]{:S(2)}) %collective-permute-start.1) | collective-permute-done | bytes 30752 | tf_op jit(solution)/shard_map/ppermute | solution.py:17
  148.6 0.3 maximum_convert_fusion
  148.9 104.4 %all-gather.5.cloned.1.call-done = bf16[1024,1024]{0,1:T(8,128)(2,1)} async-done(((bf16[1024,16]{0,1:T(8,128)(2,1)}), bf16[1024,1024]{0,1:T(8,128)(2,1)}) %all-gather.5.cloned.1.call-update) | async-done | bytes 2097168 | tf_op jit(solution)/shard_map/all_gather | solution.py:42
  253.2 0.0 copy-done.3
  253.2 0.0 copy-done.4
  253.2 11.9 %fusion.5 = bf16[512,1024]{1,0:T(8,128)(2,1)} fusion(bf16[1024,1024]{0,1:T(8,128)(2,1)} %all-gather.5.cloned.1.call-done, f32[542,1024]{1,0:T(8,128)S(1)} %maximum_convert_fusion, f32[1024]{0:T(1024)S(1)} %copy-done.3, f32[1024]{0:T(1024)S(1)} %copy-done.4, f32[1024]{0:T(1024)S(1)} %bitcast.67, f32[1024]{0:T(1024)S(1)} %bitcast.68, f32[1024]{0:T(1024)S(1)} %bitcast.39, ...), kind=kOutput, calls=%fused_computation.8 | convolution fusion | flops 1111490560 | bytes 69341696 | tf_op jit(solution)/shard_map/dot_general | solution.py:51
  (5 shorter events, 0.1 us)
Async XLA Ops:
  6.5 128.2 %copy-start = (bf16[512,1024]{1,0:T(8,128)(2,1)S(1)}, bf16[512,1024]{1,0:T(8,128)(2,1)}, u32[]{:S(2)}) copy-start(bf16[512,1024]{1,0:T(8,128)(2,1)} %param.9) | copy-start | bytes 3145732
  6.5 6.1 %copy-start.1 = (f32[31,1024]{1,0:T(8,128)S(1)}, f32[31,1024]{1,0:T(8,128)}, u32[]{:S(2)}) copy-start(f32[31,1024]{1,0:T(8,128)} %param.14) | copy-start | bytes 380932
  6.5 128.2 %copy-start.2 = (f32[1024]{0:T(1024)S(1)}, f32[1024]{0:T(1024)}, u32[]{:S(2)}) copy-start(f32[1024]{0:T(1024)} %param.12) | copy-start | bytes 12292
  6.5 128.2 %all-gather.3.cloned.1.call-start = ((), (), s32[]{:S(2)}) async-start(), calls=%async_computation | async-start | bytes 4259840 | tf_op jit(solution)/shard_map/all_gather | solution.py:41
  7.3 246.0 %all-gather.5.cloned.1.call-start = ((), (), s32[]{:S(2)}) async-start(), calls=%async_computation.1 | async-start | bytes 2129920 | tf_op jit(solution)/shard_map/all_gather | solution.py:42
  140.1 113.1 %copy-start.3 = (f32[1024]{0:T(1024)S(1)}, f32[1024]{0:T(1024)}, u32[]{:S(2)}) copy-start(f32[1024]{0:T(1024)} %param.16) | copy-start | bytes 12292
  140.1 113.1 %copy-start.4 = (f32[1024]{0:T(1024)S(1)}, f32[1024]{0:T(1024)}, u32[]{:S(2)}) copy-start(f32[1024]{0:T(1024)} %param.15) | copy-start | bytes 12292
  140.2 5.1 %collective-permute-start = (bf16[15,1024]{1,0:T(8,128)(2,1)S(1)}, bf16[15,1024]{1,0:T(8,128)(2,1)S(1)}, u32[]{:S(2)}, u32[]{:S(2)}) collective-permute-start(bf16[15,1024]{1,0:T(8,128)(2,1)S(1)} %get-tuple-element.5), channel_id=1, source_target_pairs={{0,1},{1,2},{2,3},{3,4},{4,5},{5,6},{6,7},{7,8},{8,9},{9,10},{10,1... | collective-permute-start | bytes 92168 | tf_op jit(solution)/shard_map/ppermute | solution.py:15
  143.3 5.2 %collective-permute-start.1 = (bf16[15,1024]{1,0:T(8,128)(2,1)S(1)}, bf16[15,1024]{1,0:T(8,128)(2,1)S(1)}, u32[]{:S(2)}, u32[]{:S(2)}) collective-permute-start(bf16[15,1024]{1,0:T(8,128)(2,1)S(1)} %get-tuple-element.6), channel_id=1, source_target_pairs={{1,0},{2,1},{3,2},{4,3},{5,4},{6,5},{7,6},{8,7},{9,8},{10,9},{11,1... | collective-permute-start | bytes 92168 | tf_op jit(solution)/shard_map/ppermute | solution.py:17
Sparse Core Ops, SparseCore 0:
  9.5 125.1 all-gather.2
  136.9 116.3 all-gather.4
where the time goes:
time: 272 us
  waiting for transfers between devices  231 us (85%)
  matrix products  16.7 us (6%)
  between operations  14.8 us (5%)
  starting transfers between devices  5.12 us (2%)
  other arithmetic  4.23 us (2%)
    all_gather x1, waiting for transfers between devices, shards(): lax.all_gather(w_in, 'tm', axis=1, tiled=True)  122 us
    all_gather x1, waiting for transfers between devices, shards(): lax.all_gather(w_out, 'tm', axis=1, tiled=True)  104 us
    dot_general x1, matrix products, shards(): branch = jnp.dot(activated, full_out, preferred_element_type=jnp.float32)  11.9 us
  transfers between devices with their start and end apart: 4, of which 3 were waited for; matrix products, arithmetic and copies ran while one was open for 3% of the time, Pallas kernels for 0%

commit v1 on v0

v1 whole, which is shorter than its diff:
```python
import jax
import jax.numpy as jnp
from jax import lax
from jax.experimental import pallas as pl
from jax.experimental.pallas import tpu as pltpu
from jax.sharding import PartitionSpec as P

MESH = pl.DeviceIdType.MESH
BF16, F32 = jnp.bfloat16, jnp.float32
NT = (((1,), (1,)), ((), ()))

ROWS = 512
HALO = 16
SPAN = ROWS + 2 * HALO
D = 1024
TAPS = 31
VAL = 32
OUT = 16
NX, NY, NZ = 4, 4, 8
LN_ROWS = 136
CONV_ROWS = 128


def remote(src, dst, send_sem, recv_sem, device):
    return pltpu.make_async_remote_copy(
        src_ref=src, dst_ref=dst, send_sem=send_sem, recv_sem=recv_sem, device_id=device, device_id_type=MESH
    )


def kernel(
    start_ref, length_ref, frames, w_in, w_out, gain, taps, scale, shift, out,
    fbuf, normed, win, wout, W, WO, G, conv_in, act, acc, obuf,
    local_sem, halo_s, halo_r, zin_s, zin_r, yin_s, yin_r, din_s, din_r,
    x_s, x_r, xf_s, xf_r, zo_s, zo_r, yo_s, yo_r, do_s, do_r,
):
    var, tm = lax.axis_index("var"), lax.axis_index("tm")
    y_hi, x = var // NX, lax.rem(var, NX)
    z, y_lo, core = tm // (2 * NY), lax.rem(tm // 2, NY), lax.rem(tm, 2)
    y = y_hi * NY + y_lo

    def at_y(step):
        there = lax.rem(y + step, 2 * NY)
        return ((there // NY) * NX + x, z * 2 * NY + lax.rem(there, NY) * 2 + core)

    def at_z(step):
        return (var, lax.rem(z + step, NZ) * 2 * NY + y_lo * 2 + core)

    def at_x(step):
        return (y_hi * NX + lax.rem(x + step, NX), tm)

    partner = (var, z * 2 * NY + y_lo * 2 + (1 - core))
    up = jnp.where((core == 1) & (y_lo == NY - 1), 1 - y_hi, y_hi)
    down = jnp.where((core == 0) & (y_lo == 0), 1 - y_hi, y_hi)
    after = (up * NX + x, lax.rem(tm + 1, 2 * NY * NZ))
    before = (down * NX + x, lax.rem(tm + 2 * NY * NZ - 1, 2 * NY * NZ))

    barrier = pltpu.get_barrier_semaphore()
    friends = [at_z(k) for k in range(1, NZ)] + [at_y(1), at_y(2), at_y(6), at_y(7)]
    friends += [at_x(1), at_x(3), partner, after, before]
    for device in friends:
        pl.semaphore_signal(barrier, inc=1, device_id=device, device_id_type=MESH)

    get_in = pltpu.make_async_copy(w_in, win, local_sem.at[0])
    get_out = pltpu.make_async_copy(w_out, wout, local_sem.at[1])
    get_frames = pltpu.make_async_copy(frames, fbuf.at[pl.ds(HALO, ROWS)], local_sem.at[2])
    get_in.start()
    get_out.start()
    get_frames.start()

    role = z // 4
    depth = lax.rem(z - x + NZ, NZ)
    is_source = lax.rem(depth, 4) == 0
    half = y_lo // 2
    slot = lax.rem(y_lo, 2) * 2 + core

    get_in.wait()

    @pl.when(is_source)
    def _():
        W[half, role, slot] = win[...].T

    get_out.wait()
    WO[z, y_lo, core] = wout[...].T
    get_frames.wait()
    pl.semaphore_wait(barrier, len(friends))

    own = W.at[half, role, slot]
    zin = {k: remote(own, own, zin_s.at[k], zin_r.at[role], at_z(k)) for k in range(1, NZ)}

    @pl.when(is_source)
    def _():
        for k in (4, 3, 5, 2, 6, 1, 7):
            zin[k].start()

    tail = remote(fbuf.at[pl.ds(ROWS, HALO)], fbuf.at[pl.ds(0, HALO)], halo_s.at[0], halo_r.at[0], after)
    head = remote(fbuf.at[pl.ds(HALO, HALO)], fbuf.at[pl.ds(HALO + ROWS, HALO)], halo_s.at[1], halo_r.at[1], before)
    tail.start()
    head.start()

    def normalize(row, count, keep):
        values = fbuf[pl.ds(row, count)].astype(F32)
        average = jnp.mean(values, axis=1, keepdims=True)
        centred = values - average
        variance = jnp.mean(centred * centred, axis=1, keepdims=True)
        result = centred * lax.rsqrt(variance + 1e-05) * gain[...]
        if keep is not None:
            result = jnp.where(keep, result, 0.0)
        normed[pl.ds(row, count)] = result.astype(BF16)

    for i in range(ROWS // 128):
        normalize(HALO + i * 128, 128, None)

    near = jnp.where((depth <= 2) | (depth >= 6), 0, 1)

    def yin(r, j):
        s = lax.rem(y_lo + (0, 3, 1, 2)[j], NY)
        piece = W.at[s // 2, r, lax.rem(s, 2) * 2 + core]
        return piece

    def y_copy(r, j):
        device = {1: at_y(1), 2: at_y(7), 3: at_y(2 + 4 * r)}[j]
        return remote(yin(r, 0), yin(r, 0), yin_s.at[r, j], yin_r.at[r, j], device)

    def y_arrival(r, j):
        return remote(yin(r, j), yin(r, j), yin_s.at[r, j], yin_r.at[r, j], partner)

    def core_copy(r, j):
        return remote(yin(r, j), yin(r, j), din_s.at[r, j], din_r.at[r, j], partner)

    def core_arrival(r, j):
        s = lax.rem(y_lo + (0, 3, 1, 2)[j], NY)
        piece = W.at[s // 2, r, lax.rem(s, 2) * 2 + 1 - core]
        return remote(piece, piece, din_s.at[r, j], din_r.at[r, j], partner)

    for r in (near, 1 - near):

        @pl.when(depth != 4 * r)
        def _(r=r):
            piece = yin(r, 0)
            remote(piece, piece, zin_s.at[0], zin_r.at[r], partner).wait_recv()

        for j in (3, 1, 2):
            y_copy(r, j).start()
        core_copy(r, 0).start()

    zo = {k: remote(WO.at[z, y_lo, core], WO.at[z, y_lo, core], zo_s.at[k], zo_r.at[k], at_z(k)) for k in range(1, NZ)}
    for k in (4, 3, 5, 2, 6, 1, 7):
        zo[k].start()

    tail.wait_recv()
    head.wait_recv()
    normalize(0, HALO, tm > 0)
    normalize(HALO + ROWS, HALO, tm < 2 * NY * NZ - 1)

    for j in (1, 2):
        for r in (near, 1 - near):
            y_arrival(r, j).wait_recv()
            core_copy(r, j).start()

    def lift(h):
        columns = jnp.concatenate([W[h, 0].reshape(128, D), W[h, 1].reshape(128, D)], axis=0)
        lifted = lax.dot_general(normed[...], columns, NT, preferred_element_type=F32)
        G[x, h] = (lifted[:, :128] * jax.nn.sigmoid(lifted[:, 128:])).astype(BF16)

    first, second = half, 1 - half

    def x_copy(order, way):
        h = (first, second)[order]
        return remote(G.at[x, h], G.at[x, h], x_s.at[order, way], x_r.at[order, way], at_x((1, 3)[way]))

    def x_arrival(order, way):
        piece = G.at[lax.rem(x + (3, 1)[way], NX), (first, second)[order]]
        return remote(piece, piece, x_s.at[order, way], x_r.at[order, way], partner)

    def x_forward(order):
        piece = G.at[lax.rem(x + (3, 1)[order], NX), (first, second)[order]]
        return remote(piece, piece, xf_s.at[order], xf_r.at[order], at_x((1, 3)[order]))

    def x_far(order):
        piece = G.at[lax.rem(x + 2, NX), (first, second)[order]]
        return remote(piece, piece, xf_s.at[order], xf_r.at[order], partner)

    pair = 2 - lax.rem(y_lo, 2)

    def core_wait(r, j):
        piece = W.at[half, 0, 0]
        remote(piece, piece, din_s.at[r, 0], din_r.at[r, j], partner).wait_recv()

    for r in (0, 1):
        core_arrival(r, 0).wait_recv()
    for r in (0, 1):
        core_wait(r, pair)
    lift(first)
    x_copy(0, 0).start()
    x_copy(0, 1).start()

    for r in (near, 1 - near):
        y_arrival(r, 3).wait_recv()
        core_copy(r, 3).start()
    for r in (0, 1):
        core_wait(r, 3 - pair)
    for r in (0, 1):
        core_arrival(r, 3).wait_recv()
    lift(second)
    x_copy(1, 0).start()
    x_copy(1, 1).start()

    for k in range(1, NZ):
        piece = WO.at[lax.rem(z + NZ - k, NZ), y_lo, core]
        remote(piece, piece, zo_s.at[k], zo_r.at[k], partner).wait_recv()
    line = WO.at[:, y_lo, core]
    low, high = WO.at[pl.ds(0, NZ // 2), y_lo, core], WO.at[pl.ds(NZ // 2, NZ // 2), y_lo, core]
    yo = [
        remote(line, line, yo_s.at[0], yo_r.at[0], at_y(1)),
        remote(line, line, yo_s.at[1], yo_r.at[1], at_y(7)),
        remote(low, low, yo_s.at[2], yo_r.at[2], at_y(2)),
        remote(high, high, yo_s.at[3], yo_r.at[3], at_y(6)),
    ]
    for copy in yo:
        copy.start()

    def out_line(j, c):
        return WO.at[:, lax.rem(y_lo + (0, 3, 1, 2)[j], NY), c]

    def do(j):
        return remote(out_line(j, core), out_line(j, core), do_s.at[j], do_r.at[j], partner)

    do(0).start()

    row0 = tm * ROWS
    span_low, span_high = start_ref[0], start_ref[0] + length_ref[0]

    def occluded(begin, count):
        position = begin + lax.broadcasted_iota(jnp.int32, (count, 1), 0)
        return (position >= span_low) & (position < span_high)

    def convolve(step, order):
        owner, h = lax.rem(x + step, NX), (first, second)[order]
        lanes = pl.ds(pl.multiple_of(owner * 256 + h * 128, 128), 128)
        conv_in[...] = jnp.where(occluded(row0 - HALO, SPAN), 0.0, G[owner, h].astype(F32))

        @pl.loop(0, ROWS // CONV_ROWS)
        def _(i):
            row = pl.multiple_of(i * CONV_ROWS, CONV_ROWS)
            total = None
            for j in range(TAPS):
                term = conv_in[pl.ds(row + j + 1, CONV_ROWS)] * taps[pl.ds(j, 1), lanes]
                total = term if total is None else total + term
            value = total * scale[:, lanes] + shift[:, lanes]
            act[owner, pl.ds(row, CONV_ROWS), pl.ds(pl.multiple_of(h * 128, 128), 128)] = (
                value * jax.nn.sigmoid(value)
            ).astype(BF16)

    def product(step, n):
        owner = lax.rem(x + step, NX)
        depths = pl.ds(pl.multiple_of(owner * 256, 256), 256)
        columns = WO[2 * n : 2 * n + 2, :, :, :, depths].reshape(256, 256)
        return lax.dot_general(act[owner], columns, NT, preferred_element_type=F32)

    convolve(0, 0)
    convolve(0, 1)

    x_arrival(0, 0).wait_recv()
    x_forward(0).start()
    convolve(3, 0)
    x_arrival(0, 1).wait_recv()
    convolve(1, 0)

    for j in (1, 2):
        remote(out_line(j, core), out_line(j, core), yo_s.at[0], yo_r.at[j - 1], partner).wait_recv()
        do(j).start()

    x_arrival(1, 1).wait_recv()
    x_forward(1).start()
    convolve(1, 1)
    x_arrival(1, 0).wait_recv()
    convolve(3, 1)

    far = lax.rem(y_lo + 2, NY)
    for part in (0, 1):
        piece = WO.at[pl.ds(part * 4, 4), far, core]
        remote(piece, piece, yo_s.at[0], yo_r.at[2 + part], partner).wait_recv()
    do(3).start()
    for j in range(4):
        remote(out_line(j, 1 - core), out_line(j, 1 - core), do_s.at[j], do_r.at[j], partner).wait_recv()

    for n in range(4):
        acc[n] = product(0, n)
    for step in (1, 3):
        for n in range(4):
            acc[n] += product(step, n)

    for order in (0, 1):
        x_far(order).wait_recv()
        convolve(2, order)

    results = []
    for n in range(4):
        lanes = pl.ds(n * 256, 256)
        masked = jnp.where(occluded(row0, ROWS), 0.0, fbuf[pl.ds(HALO, ROWS), lanes].astype(F32))
        obuf[:, lanes] = (masked + (acc[n] + product(2, n))).astype(BF16)
        copy = pltpu.make_async_copy(obuf.at[:, lanes], out.at[:, lanes], local_sem.at[3 + n])
        copy.start()
        results.append(copy)

    @pl.when(is_source)
    def _():
        for k in range(1, NZ):
            zin[k].wait_send()

    tail.wait_send()
    head.wait_send()
    for r in (0, 1):
        for j in (1, 2, 3):
            y_copy(r, j).wait_send()
        for j in range(4):
            core_copy(r, j).wait_send()
    for order in (0, 1):
        for way in (0, 1):
            x_copy(order, way).wait_send()
        x_forward(order).wait_send()
    for k in range(1, NZ):
        zo[k].wait_send()
    for copy in yo:
        copy.wait_send()
    for j in range(4):
        do(j).wait_send()
    for copy in results:
        copy.wait()


def module(frames, span_start, span_length, ln_gain, w_in, taps, bn_scale, bn_shift, w_out):
    vmem, smem, hbm = (pl.BlockSpec(memory_space=space) for space in (pltpu.VMEM, pltpu.SMEM, pl.ANY))
    dma = pltpu.SemaphoreType.DMA
    return pl.pallas_call(
        kernel,
        name="conformer_conv",
        out_shape=jax.ShapeDtypeStruct((ROWS, D), BF16),
        in_specs=[smem, smem, hbm, hbm, hbm, vmem, vmem, vmem, vmem],
        out_specs=hbm,
        scratch_shapes=[
            pltpu.VMEM((SPAN, D), BF16),
            pltpu.VMEM((SPAN, D), BF16),
            pltpu.VMEM((D, VAL), BF16),
            pltpu.VMEM((D, OUT), BF16),
            pltpu.VMEM((2, 2, 4, VAL, D), BF16),
            pltpu.VMEM((NZ, NY, 2, OUT, D), BF16),
            pltpu.VMEM((NX, 2, SPAN, 128), BF16),
            pltpu.VMEM((SPAN, 128), F32),
            pltpu.VMEM((NX, ROWS, 256), BF16),
            pltpu.VMEM((4, ROWS, 256), F32),
            pltpu.VMEM((ROWS, D), BF16),
            dma((7,)),
            dma((2,)), dma((2,)),
            dma((NZ,)), dma((2,)),
            dma((2, 4)), dma((2, 4)),
            dma((2, 4)), dma((2, 4)),
            dma((2, 2)), dma((2, 2)),
            dma((2,)), dma((2,)),
            dma((NZ,)), dma((NZ,)),
            dma((4,)), dma((4,)),
            dma((4,)), dma((4,)),
        ],
        compiler_params=pltpu.CompilerParams(
            collective_id=0, has_side_effects=True, vmem_limit_bytes=40 * 1024 * 1024
        ),
    )(
        span_start, span_length, frames, w_in, w_out, ln_gain.reshape(1, D), taps,
        bn_scale.reshape(1, D), bn_shift.reshape(1, D),
    )


def solution(mesh):
    return jax.shard_map(
        module,
        mesh=mesh,
        in_specs=(P("tm", None), P("var"), P("var"), P(), P(None, "tm"), P(), P(), P(), P(None, "tm")),
        out_specs=P(("var", "tm"), None),
        check_vma=False,
    )
```

time: 272 us -> 57.3 us (0.21)
  the two profiles are of different devices: /device:TPU:1 before, /device:TPU:3 now
where the time goes in v1:
time: 57.3 us; the launch traced here: 57 us
  Pallas kernels  51.6 us (90%)
  local copies, waits for them, and re-layouts  4.09 us (7%)
  between operations  1.37 us (2%)
    pallas_call x1, Pallas kernels, module(): pl.pallas_call(kernel, name='conformer_conv', out_shape=jax.ShapeDtypeStr...  51.6 us
    unnamed x15, local copies, waits for them, and re-layouts  4.09 us

profile of v1, /device:TPU:3, one launch (start us, length us, event | category | flops | bytes accessed | tf_op | source)
XLA Modules:
  0.0 57.0 jit_solution(2754205993376932933)
XLA Ops:
  1.3 0.0 copy-start.5
  1.3 1.0 %copy.10.w_in = bf16[1024,32]{1,0:T(8,128)(2,1)S(1)} copy(bf16[1024,32]{0,1:T(8,128)(2,1)} %param.13) | data formatting | bytes 131072 | tf_op args[4]
  2.3 0.0 copy-done.5
  2.3 0.0 copy-start.1
  2.3 0.0 copy-start.2
  2.4 0.0 copy-start.3
  2.4 0.0 copy-start.4
  2.4 0.2 copy.11.w_out
  2.6 0.7 %copy-done.1 = f32[31,1024]{1,0:T(8,128)S(1)} copy-done((f32[31,1024]{1,0:T(8,128)S(1)}, f32[31,1024]{1,0:T(8,128)}, u32[]{:S(2)}) %copy-start.1) | copy-done | bytes 127000
  3.2 0.0 copy-done.2
  3.2 0.0 copy-done.3
  3.2 0.0 copy-done.4
  3.3 0.0 copy-start
  3.3 1.2 %copy-done = bf16[512,1024]{1,0:T(8,128)(2,1)S(1)} copy-done((bf16[512,1024]{1,0:T(8,128)(2,1)S(1)}, bf16[512,1024]{1,0:T(8,128)(2,1)}, u32[]{:S(2)}) %copy-start) | copy-done | bytes 1048600
  4.5 51.6 %conformer_conv.1 = bf16[512,1024]{1,0:T(8,128)(2,1)S(1)} custom-call(s32[1]{0:T(128)S(6)} %copy.13.start_ref, s32[1]{0:T(128)S(6)} %copy.14.length_ref, bf16[512,1024]{1,0:T(8,128)(2,1)S(1)} %copy-done, bf16[1024,32]{1,0:T(8,128)(2,1)S(1)} %copy.10.w_in, bf16[1024,16]{1,0:T(8,128)(2,1)S(1)} %copy.11.w_out, f32[1,1024]{1,0:T(1,128)S(1)} %bitcast.3, ...), custom_call_target="tpu_custom_call" | custom-call | tf_op jit(solution)/shard_map/conformer_conv/pallas_call | solution.py:335
  56.1 1.0 %copy.15 = bf16[512,1024]{1,0:T(8,128)(2,1)} copy(bf16[512,1024]{1,0:T(8,128)(2,1)S(1)} %conformer_conv.1) | data formatting | bytes 2097152
Async XLA Ops:
  1.3 1.0 %copy-start.5 = (bf16[1024,16]{0,1:T(8,128)(2,1)S(1)}, bf16[1024,16]{0,1:T(8,128)(2,1)}, u32[]{:S(2)}) copy-start(bf16[1024,16]{0,1:T(8,128)(2,1)} %param.17) | copy-start | bytes 98308
  2.3 0.9 %copy-start.1 = (f32[31,1024]{1,0:T(8,128)S(1)}, f32[31,1024]{1,0:T(8,128)}, u32[]{:S(2)}) copy-start(f32[31,1024]{1,0:T(8,128)} %taps.1) | copy-start | bytes 380932
  2.3 0.9 %copy-start.2 = (f32[1024]{0:T(1024)S(1)}, f32[1024]{0:T(1024)}, u32[]{:S(2)}) copy-start(f32[1024]{0:T(1024)} %param.12) | copy-start | bytes 12292
  2.4 0.9 %copy-start.3 = (f32[1024]{0:T(1024)S(1)}, f32[1024]{0:T(1024)}, u32[]{:S(2)}) copy-start(f32[1024]{0:T(1024)} %param.15) | copy-start | bytes 12292
  2.4 0.9 %copy-start.4 = (f32[1024]{0:T(1024)S(1)}, f32[1024]{0:T(1024)}, u32[]{:S(2)}) copy-start(f32[1024]{0:T(1024)} %param.16) | copy-start | bytes 12292
  3.3 1.2 %copy-start = (bf16[512,1024]{1,0:T(8,128)(2,1)S(1)}, bf16[512,1024]{1,0:T(8,128)(2,1)}, u32[]{:S(2)}) copy-start(bf16[512,1024]{1,0:T(8,128)(2,1)} %frames.1) | copy-start | bytes 3145732

commit v2 on v1

v2 whole, which is shorter than its diff:
```python
import jax
import jax.numpy as jnp
from jax import lax
from jax.experimental import pallas as pl
from jax.experimental.pallas import tpu as pltpu
from jax.sharding import PartitionSpec as P

MESH = pl.DeviceIdType.MESH
BF16, F32 = jnp.bfloat16, jnp.float32
NT = (((1,), (1,)), ((), ()))

ROWS = 512
HALO = 16
SPAN = ROWS + 2 * HALO
D = 1024
TAPS = 31
VAL = 32
OUT = 16
NX, NY, NZ = 4, 4, 8
LB = 384
VMEM_BYTES = 58 * 1024 * 1024
CONV_ROWS = 128


def remote(src, dst, send_sem, recv_sem, device):
    return pltpu.make_async_remote_copy(
        src_ref=src, dst_ref=dst, send_sem=send_sem, recv_sem=recv_sem, device_id=device, device_id_type=MESH
    )


def kernel(
    start_hbm, length_hbm, frames, w_in, w_out, gain_hbm, taps_hbm, scale_hbm, shift_hbm, out,
    fbuf, normed, win, wout, W, WO, G, conv_in, act, acc, obuf, gain, raw_taps, raw_scale, raw_shift, params, start, length,
    local_sem, halo_s, halo_r, zin_s, zin_r, yin_s, yin_r, din_s, din_r,
    x_s, x_r, xf_s, xf_r, zo_s, zo_r, xo_s, xo_r, yo_s, yo_r, do_s, do_r,
    yb_s, yb_r, zb_s, zb_r, db_s, db_r,
):
    var, tm = lax.axis_index("var"), lax.axis_index("tm")
    y_hi, x = var // NX, lax.rem(var, NX)
    z, y_lo, core = tm // (2 * NY), lax.rem(tm // 2, NY), lax.rem(tm, 2)
    y = y_hi * NY + y_lo

    def at_y(step):
        there = lax.rem(y + step, 2 * NY)
        return ((there // NY) * NX + x, z * 2 * NY + lax.rem(there, NY) * 2 + core)

    def at_z(step):
        return (var, lax.rem(z + step, NZ) * 2 * NY + y_lo * 2 + core)

    def at_x(step):
        return (y_hi * NX + lax.rem(x + step, NX), tm)

    partner = (var, z * 2 * NY + y_lo * 2 + (1 - core))
    up = jnp.where((core == 1) & (y_lo == NY - 1), 1 - y_hi, y_hi)
    down = jnp.where((core == 0) & (y_lo == 0), 1 - y_hi, y_hi)
    after = (up * NX + x, lax.rem(tm + 1, 2 * NY * NZ))
    before = (down * NX + x, lax.rem(tm + 2 * NY * NZ - 1, 2 * NY * NZ))

    barrier = pltpu.get_barrier_semaphore()
    friends = [at_z(k) for k in (4, 3, 5, 2, 6, 1, 7)] + [at_y(2), at_y(6), at_y(1), at_y(7)]
    friends += [at_x(2), at_x(1), at_x(3), after, before, partner]
    for device in friends:
        pl.semaphore_signal(barrier, inc=1, device_id=device, device_id_type=MESH)

    fetch = [
        pltpu.make_async_copy(src, dst, local_sem.at[i])
        for i, (src, dst) in enumerate(
            (
                (w_in, win),
                (w_out, wout),
                (frames, fbuf.at[pl.ds(HALO, ROWS)]),
                (taps_hbm, raw_taps),
                (scale_hbm, raw_scale),
                (shift_hbm, raw_shift),
                (gain_hbm, gain),
                (start_hbm, start),
                (length_hbm, length),
            )
        )
    ]
    for copy in fetch:
        copy.start()

    role = z // 4
    depth = lax.rem(z - x + NZ, NZ)
    is_source = lax.rem(depth, 4) == 0

    old = lax.broadcasted_iota(jnp.int32, (256, 256), 0)
    new = lax.broadcasted_iota(jnp.int32, (256, 256), 1)
    order = (old // 32 == (new // 16) % 8) & ((old // 16) % 2 == new // 128) & (old % 16 == new % 16)
    order = jnp.where(order, 1.0, 0.0)

    fetch[0].wait()

    @pl.when(is_source)
    def _():
        W[0, role, y_lo, core] = win[:16]
        W[1, role, y_lo, core] = win[16:]

    fetch[1].wait()
    for b in range(4):
        lanes = pl.ds(b * 256, 256)
        wout[:, lanes] = jnp.dot(wout[:, lanes], order.astype(BF16), preferred_element_type=F32).astype(BF16)
    WO[z, y_lo, core, :, :LB] = wout[:, :LB]

    @pl.when(is_source)
    def _():
        WO[z, y_lo, core, :, LB:] = wout[:, LB:]

    fetch[2].wait()
    pl.semaphore_wait(barrier, len(friends))

    back = pl.ds(LB, D - LB)
    front = pl.ds(0, LB)
    far_first = (4, 3, 5, 2, 6, 1, 7)

    def zin(c, k):
        piece = W.at[c, role, y_lo, core]
        return remote(piece, piece, zin_s.at[c, k], zin_r.at[c, role], at_z(k))

    def zo(k):
        piece = WO.at[z, y_lo, core, :, back]
        return remote(piece, piece, zo_s.at[k], zo_r.at[role], at_z(k))

    @pl.when(is_source)
    def _():
        for c in (0, 1):
            for k in far_first:
                zin(c, k).start()
        for k in far_first:
            zo(k).start()

    def yb(j):
        piece = WO.at[z, y_lo, core, :, front]
        return remote(piece, piece, yb_s.at[j], yb_r.at[j], at_y((0, 1, 7, 2)[j]))

    for j in (3, 1, 2):
        yb(j).start()

    tail = remote(fbuf.at[pl.ds(ROWS, HALO)], fbuf.at[pl.ds(0, HALO)], halo_s.at[0], halo_r.at[0], after)
    head = remote(fbuf.at[pl.ds(HALO, HALO)], fbuf.at[pl.ds(HALO + ROWS, HALO)], halo_s.at[1], halo_r.at[1], before)
    tail.start()
    head.start()

    for copy in fetch[3:]:
        copy.wait()
    for b in range(4):
        lanes = pl.ds(b * 256, 256)
        for first, src in ((0, raw_taps), (32, raw_scale), (40, raw_shift)):
            params[pl.ds(first, src.shape[0]), lanes] = jnp.dot(
                src[:, lanes], order, precision=lax.Precision.HIGHEST, preferred_element_type=F32
            )

    def normalize(row, count, keep):
        values = fbuf[pl.ds(row, count)].astype(F32)
        average = jnp.mean(values, axis=1, keepdims=True)
        centred = values - average
        variance = jnp.mean(centred * centred, axis=1, keepdims=True)
        result = centred * lax.rsqrt(variance + 1e-05) * gain[...]
        if keep is not None:
            result = jnp.where(keep, result, 0.0)
        normed[pl.ds(row, count)] = result.astype(BF16)

    for i in range(ROWS // 128):
        normalize(HALO + i * 128, 128, None)
    tail.wait_recv()
    head.wait_recv()
    normalize(0, HALO, tm > 0)
    normalize(HALO + ROWS, HALO, tm < 2 * NY * NZ - 1)

    near = jnp.where((depth <= 2) | (depth >= 6), 0, 1)
    roles = (near, 1 - near)

    def line(j):
        return lax.rem(y_lo + (0, 3, 1, 2)[j], NY)

    def yin(c, r, j):
        piece = W.at[c, r, y_lo, core]
        device = {1: at_y(1), 2: at_y(7), 3: at_y(2 + 4 * r)}[j]
        return remote(piece, piece, yin_s.at[c, r, j], yin_r.at[c, r, j], device)

    def yin_arrival(c, r, j):
        piece = W.at[c, r, line(j), core]
        return remote(piece, piece, yin_s.at[c, r, j], yin_r.at[c, r, j], partner)

    def din(c, r, j):
        piece = W.at[c, r, line(j), core]
        return remote(piece, piece, din_s.at[c, r, j], din_r.at[c, r, j], partner)

    def din_arrival(c, r, j):
        piece = W.at[c, r, line(j), 1 - core]
        return remote(piece, piece, din_s.at[c, r, j], din_r.at[c, r, j], partner)

    for c in (0, 1):
        for r in roles:

            @pl.when(depth != 4 * r)
            def _(c=c, r=r):
                piece = W.at[c, r, y_lo, core]
                remote(piece, piece, zin_s.at[c, 0], zin_r.at[c, r], partner).wait_recv()

            for j in (3, 1, 2):
                yin(c, r, j).start()
            din(c, r, 0).start()

    def xo(r, w):
        piece = WO.at[x + 4 * r, y_lo, core, :, back]
        return remote(piece, piece, xo_s.at[r, w], xo_r.at[r, w], at_x((2, 1, 3)[w]))

    for r in (0, 1):

        @pl.when(depth != 4 * r)
        def _(r=r):
            piece = WO.at[x + 4 * r, y_lo, core, :, back]
            remote(piece, piece, zo_s.at[0], zo_r.at[r], partner).wait_recv()

        for w in range(3):
            xo(r, w).start()

    for j in (1, 2, 3):
        piece = WO.at[z, line(j), core, :, front]
        remote(piece, piece, yb_s.at[j], yb_r.at[j], partner).wait_recv()

    def zb(k):
        piece = WO.at[z, :, core, :, front]
        return remote(piece, piece, zb_s.at[k], zb_r.at[k], at_z(k))

    for k in far_first:
        zb(k).start()

    def lift(c):
        columns = jnp.concatenate([W[c, 0].reshape(128, D), W[c, 1].reshape(128, D)], axis=0)
        lifted = lax.dot_general(normed[...], columns, NT, preferred_element_type=F32)
        G[x, c] = (lifted[:, :128] * jax.nn.sigmoid(lifted[:, 128:])).astype(BF16)

    parts = (pl.ds(0, SPAN // 2), pl.ds(SPAN // 2, SPAN // 2))

    def x_copy(c, way, p):
        piece = G.at[x, c, parts[p]]
        return remote(piece, piece, x_s.at[c, way, p], x_r.at[c, way, p], at_x((1, 3)[way]))

    def x_arrival(c, way, p):
        piece = G.at[lax.rem(x + (3, 1)[way], NX), c, parts[p]]
        return remote(piece, piece, x_s.at[c, way, p], x_r.at[c, way, p], partner)

    def x_forward(c, p):
        piece = G.at[lax.rem(x + (3, 1)[p], NX), c, parts[p]]
        return remote(piece, piece, xf_s.at[c, p], xf_r.at[c, p], at_x((1, 3)[p]))

    def x_far(c, p):
        piece = G.at[lax.rem(x + 2, NX), c, parts[p]]
        return remote(piece, piece, xf_s.at[c, p], xf_r.at[c, p], partner)

    def lift_and_send(c):
        for j in (1, 2, 3):
            for r in roles:
                yin_arrival(c, r, j).wait_recv()
                din(c, r, j).start()
        for j in range(4):
            for r in (0, 1):
                din_arrival(c, r, j).wait_recv()
        lift(c)
        for p in (0, 1):
            for way in (0, 1):
                x_copy(c, way, p ^ way).start()

    lift_and_send(0)

    for w in range(3):
        for r in (0, 1):
            piece = WO.at[lax.rem(x + (2, 3, 1)[w], NX) + 4 * r, y_lo, core, :, back]
            remote(piece, piece, xo_s.at[r, w], xo_r.at[r, w], partner).wait_recv()

    full = WO.at[:, y_lo, core, :, back]
    low, high = WO.at[pl.ds(0, NZ // 2), y_lo, core, :, back], WO.at[pl.ds(NZ // 2, NZ // 2), y_lo, core, :, back]
    yo = [
        remote(low, low, yo_s.at[2], yo_r.at[2], at_y(2)),
        remote(high, high, yo_s.at[3], yo_r.at[3], at_y(6)),
        remote(full, full, yo_s.at[0], yo_r.at[0], at_y(1)),
        remote(full, full, yo_s.at[1], yo_r.at[1], at_y(7)),
    ]
    for copy in yo:
        copy.start()

    def do(j):
        piece = WO.at[:, line(j), core, :, back]
        return remote(piece, piece, do_s.at[j], do_r.at[j], partner)

    do(0).start()

    lift_and_send(1)

    row0 = tm * ROWS
    span_low, span_high = start[0], start[0] + length[0]

    def occluded(begin, count):
        position = begin + lax.broadcasted_iota(jnp.int32, (count, 1), 0)
        return (position >= span_low) & (position < span_high)

    def convolve(step, c):
        owner = lax.rem(x + step, NX)
        lanes = pl.ds(pl.multiple_of(owner * 256 + c * 128, 128), 128)
        conv_in[...] = jnp.where(occluded(row0 - HALO, SPAN), 0.0, G[owner, c].astype(F32))

        @pl.loop(0, ROWS // CONV_ROWS)
        def _(i):
            row = pl.multiple_of(i * CONV_ROWS, CONV_ROWS)
            total = None
            for j in range(TAPS):
                term = conv_in[pl.ds(row + j + 1, CONV_ROWS)] * params[pl.ds(j, 1), lanes]
                total = term if total is None else total + term
            value = total * params[pl.ds(32, 1), lanes] + params[pl.ds(40, 1), lanes]
            act[owner, pl.ds(row, CONV_ROWS), pl.ds(c * 128, 128)] = (value * jax.nn.sigmoid(value)).astype(BF16)

    def product(step, n):
        owner = lax.rem(x + step, NX)
        depths = pl.ds(pl.multiple_of(owner * 256, 256), 256)
        columns = WO[2 * n : 2 * n + 2, :, :, :, depths].reshape(256, 256)
        return lax.dot_general(act[owner], columns, NT, preferred_element_type=F32)

    convolve(0, 0)
    convolve(0, 1)
    for p in (0, 1):
        x_arrival(0, p, p).wait_recv()
        x_forward(0, p).start()
    for p in (0, 1):
        x_arrival(0, p, 1 - p).wait_recv()
    convolve(1, 0)
    convolve(3, 0)

    for p in (0, 1):
        x_arrival(1, p, p).wait_recv()
        x_forward(1, p).start()

    for k in range(1, NZ):
        piece = WO.at[lax.rem(z + NZ - k, NZ), :, core, :, front]
        remote(piece, piece, zb_s.at[k], zb_r.at[k], partner).wait_recv()
    mine = WO.at[:, :, core, :, front]
    db = remote(mine, mine, db_s.at[0], db_r.at[0], partner)
    db.start()

    for p in (0, 1):
        x_arrival(1, p, 1 - p).wait_recv()
    convolve(1, 1)
    convolve(3, 1)

    for j in (1, 2):
        piece = WO.at[:, line(j), core, :, back]
        remote(piece, piece, yo_s.at[0], yo_r.at[j - 1], partner).wait_recv()
        do(j).start()
    for h in (0, 1):
        piece = WO.at[pl.ds(h * 4, 4), line(3), core, :, back]
        remote(piece, piece, yo_s.at[0], yo_r.at[2 + h], partner).wait_recv()
    do(3).start()

    for p in (0, 1):
        x_far(0, p).wait_recv()
    convolve(2, 0)

    for j in range(4):
        piece = WO.at[:, line(j), 1 - core, :, back]
        remote(piece, piece, do_s.at[j], do_r.at[j], partner).wait_recv()
    theirs = WO.at[:, :, 1 - core, :, front]
    remote(theirs, theirs, db_s.at[0], db_r.at[0], partner).wait_recv()

    for n in range(4):
        acc[n] = product(0, n)
    for step in (1, 3):
        for n in range(4):
            acc[n] += product(step, n)

    for p in (0, 1):
        x_far(1, p).wait_recv()
    convolve(2, 1)

    results = []
    for n in range(4):
        lanes = pl.ds(n * 256, 256)
        masked = jnp.where(occluded(row0, ROWS), 0.0, fbuf[pl.ds(HALO, ROWS), lanes].astype(F32))
        obuf[:, lanes] = (masked + (acc[n] + product(2, n))).astype(BF16)
        copy = pltpu.make_async_copy(obuf.at[:, lanes], out.at[:, lanes], local_sem.at[9 + n])
        copy.start()
        results.append(copy)

    @pl.when(is_source)
    def _():
        for k in far_first:
            zin(0, k).wait_send()
            zin(1, k).wait_send()
            zo(k).wait_send()

    tail.wait_send()
    head.wait_send()
    for c in (0, 1):
        for r in (0, 1):
            for j in (1, 2, 3):
                yin(c, r, j).wait_send()
            for j in range(4):
                din(c, r, j).wait_send()
        for p in (0, 1):
            for way in (0, 1):
                x_copy(c, way, p).wait_send()
            x_forward(c, p).wait_send()
    for r in (0, 1):
        for w in range(3):
            xo(r, w).wait_send()
    for j in (1, 2, 3):
        yb(j).wait_send()
    for k in far_first:
        zb(k).wait_send()
    for copy in yo:
        copy.wait_send()
    for j in range(4):
        do(j).wait_send()
    db.wait_send()
    for copy in results:
        copy.wait()


def module(frames, span_start, span_length, ln_gain, w_in, taps, bn_scale, bn_shift, w_out):
    hbm = pl.BlockSpec(memory_space=pl.ANY)
    dma = pltpu.SemaphoreType.DMA
    return pl.pallas_call(
        kernel,
        name="conformer_conv",
        out_shape=jax.ShapeDtypeStruct((ROWS, D), BF16),
        in_specs=[hbm] * 9,
        out_specs=hbm,
        scratch_shapes=[
            pltpu.VMEM((SPAN, D), BF16),
            pltpu.VMEM((SPAN, D), BF16),
            pltpu.VMEM((VAL, D), BF16),
            pltpu.VMEM((OUT, D), BF16),
            pltpu.VMEM((2, 2, NY, 2, OUT, D), BF16),
            pltpu.VMEM((NZ, NY, 2, OUT, D), BF16),
            pltpu.VMEM((NX, 2, SPAN, 128), BF16),
            pltpu.VMEM((SPAN, 128), F32),
            pltpu.VMEM((NX, ROWS, 256), BF16),
            pltpu.VMEM((4, ROWS, 256), F32),
            pltpu.VMEM((ROWS, D), BF16),
            pltpu.VMEM((1, D), F32),
            pltpu.VMEM((TAPS, D), F32),
            pltpu.VMEM((1, D), F32),
            pltpu.VMEM((1, D), F32),
            pltpu.VMEM((48, D), F32),
            pltpu.SMEM((1,), jnp.int32),
            pltpu.SMEM((1,), jnp.int32),
            dma((13,)),
            dma((2,)), dma((2,)),
            dma((2, NZ)), dma((2, 2)),
            dma((2, 2, 4)), dma((2, 2, 4)),
            dma((2, 2, 4)), dma((2, 2, 4)),
            dma((2, 2, 2)), dma((2, 2, 2)),
            dma((2, 2)), dma((2, 2)),
            dma((NZ,)), dma((2,)),
            dma((2, 3)), dma((2, 3)),
            dma((4,)), dma((4,)),
            dma((4,)), dma((4,)),
            dma((4,)), dma((4,)),
            dma((NZ,)), dma((NZ,)),
            dma((1,)), dma((1,)),
        ],
        compiler_params=pltpu.CompilerParams(
            collective_id=0, has_side_effects=True, vmem_limit_bytes=VMEM_BYTES
        ),
    )(
        span_start, span_length, frames, w_in.T, w_out.T, ln_gain.reshape(1, D), taps,
        bn_scale.reshape(1, D), bn_shift.reshape(1, D),
    )


def solution(mesh):
    return jax.shard_map(
        module,
        mesh=mesh,
        in_specs=(P("tm", None), P("var"), P("var"), P(), P(None, "tm"), P(), P(), P(), P(None, "tm")),
        out_specs=P(("var", "tm"), None),
        check_vma=False,
    )
```

time: 57.3 us -> 47.6 us (0.83)
  the two profiles are of different devices: /device:TPU:3 before, /device:TPU:1 now
where the time goes in v2:
time: 47.6 us; the launch traced here: 47.4 us
  Pallas kernels  43.8 us (92%)
  local copies, waits for them, and re-layouts  2.26 us (5%)
  between operations  1.3 us (3%)
    pallas_call x1, Pallas kernels, module(): pl.pallas_call(kernel, name='conformer_conv', out_shape=jax.ShapeDtypeStr...  43.8 us
    unnamed x1, local copies, waits for them, and re-layouts  2.26 us

profile of v2, /device:TPU:1, one launch (start us, length us, event | category | flops | bytes accessed | tf_op | source)
XLA Modules:
  0.0 47.4 jit_solution(13612845534734178759)
XLA Ops:
  1.3 43.8 %conformer_conv.1 = bf16[512,1024]{1,0:T(8,128)(2,1)} custom-call(s32[1]{0:T(128)S(6)} %copy.11.start_hbm, s32[1]{0:T(128)S(6)} %copy.12.length_hbm, bf16[512,1024]{1,0:T(8,128)(2,1)} %frames.1, bf16[32,1024]{1,0:T(8,128)(2,1)} %bitcast.5, bf16[16,1024]{1,0:T(8,128)(2,1)} %bitcast.6, f32[1,1024]{1,0:T(1,128)} %bitcast.7, f32[31,1024]{1,0:T(8,128)} %taps_hbm.1, ...), custom_call_target="tpu_custom_call" | custom-call | tf_op jit(solution)/shard_map/conformer_conv/pallas_call | solution.py:423
  45.1 2.3 %copy.13 = bf16[512,1024]{1,0:T(8,128)(2,1)} copy(bf16[512,1024]{1,0:T(8,128)(2,1)} %conformer_conv.1) | data formatting | bytes 2097152

commit v3 on v2

--- a/solution.py
+++ b/solution.py
@@ -30,7 +30,7 @@
 
 def kernel(
     start_hbm, length_hbm, frames, w_in, w_out, gain_hbm, taps_hbm, scale_hbm, shift_hbm, out,
-    fbuf, normed, win, wout, W, WO, G, conv_in, act, acc, obuf, gain, raw_taps, raw_scale, raw_shift, params, start, length,
+    fbuf, normed, win, wout, W, WO, G, conv_in, act, acc, gain, raw_taps, raw_scale, raw_shift, params, start, length,
     local_sem, halo_s, halo_r, zin_s, zin_r, yin_s, yin_r, din_s, din_r,
     x_s, x_r, xf_s, xf_r, zo_s, zo_r, xo_s, xo_r, yo_s, yo_r, do_s, do_r,
     yb_s, yb_r, zb_s, zb_r, db_s, db_r,
@@ -373,14 +373,10 @@
         x_far(1, p).wait_recv()
     convolve(2, 1)
 
-    results = []
     for n in range(4):
         lanes = pl.ds(n * 256, 256)
         masked = jnp.where(occluded(row0, ROWS), 0.0, fbuf[pl.ds(HALO, ROWS), lanes].astype(F32))
-        obuf[:, lanes] = (masked + (acc[n] + product(2, n))).astype(BF16)
-        copy = pltpu.make_async_copy(obuf.at[:, lanes], out.at[:, lanes], local_sem.at[9 + n])
-        copy.start()
-        results.append(copy)
+        out[:, lanes] = (masked + (acc[n] + product(2, n))).astype(BF16)
 
     @pl.when(is_source)
     def _():
@@ -413,8 +409,6 @@
     for j in range(4):
         do(j).wait_send()
     db.wait_send()
-    for copy in results:
-        copy.wait()
 
 
 def module(frames, span_start, span_length, ln_gain, w_in, taps, bn_scale, bn_shift, w_out):
@@ -423,9 +417,9 @@
     return pl.pallas_call(
         kernel,
         name="conformer_conv",
-        out_shape=jax.ShapeDtypeStruct((ROWS, D), BF16),
+        out_shape=pltpu.VMEM((ROWS, D), BF16),
         in_specs=[hbm] * 9,
-        out_specs=hbm,
+        out_specs=pl.BlockSpec(memory_space=pltpu.VMEM),
         scratch_shapes=[
             pltpu.VMEM((SPAN, D), BF16),
             pltpu.VMEM((SPAN, D), BF16),
@@ -437,7 +431,6 @@
             pltpu.VMEM((SPAN, 128), F32),
             pltpu.VMEM((NX, ROWS, 256), BF16),
             pltpu.VMEM((4, ROWS, 256), F32),
-            pltpu.VMEM((ROWS, D), BF16),
             pltpu.VMEM((1, D), F32),
             pltpu.VMEM((TAPS, D), F32),
             pltpu.VMEM((1, D), F32),
@@ -445,7 +438,7 @@
             pltpu.VMEM((48, D), F32),
             pltpu.SMEM((1,), jnp.int32),
             pltpu.SMEM((1,), jnp.int32),
-            dma((13,)),
+            dma((9,)),
             dma((2,)), dma((2,)),
             dma((2, NZ)), dma((2, 2)),
             dma((2, 2, 4)), dma((2, 2, 4)),

time: 47.6 us -> 45.5 us (0.956)
  local copies, waits for them, and re-layouts: 2.26 us -> 0.97 us
  Pallas kernels: 43.8 us -> 43.1 us
    unnamed x1, local copies, waits for them, and re-layouts: 2.26 us -> 0.97 us
    pallas_call x1, Pallas kernels: 43.8 us -> 43.1 us  [module(): pl.pallas_call(kernel, name='conformer_conv', out_shape=pltpu.VMEM((ROWS,...]
where the time goes in v3:
time: 45.5 us; the launch traced here: 45.3 us
  Pallas kernels  43.1 us (95%)
  between operations  1.3 us (3%)
  local copies, waits for them, and re-layouts  0.97 us (2%)
    pallas_call x1, Pallas kernels, module(): pl.pallas_call(kernel, name='conformer_conv', out_shape=pltpu.VMEM((ROWS,...  43.1 us
    unnamed x1, local copies, waits for them, and re-layouts  0.97 us

profile of v3, /device:TPU:1, one launch (start us, length us, event | category | flops | bytes accessed | tf_op | source)
XLA Modules:
  0.0 45.3 jit_solution(13001676847892287809)
XLA Ops:
  1.3 43.1 %conformer_conv.1 = bf16[512,1024]{1,0:T(8,128)(2,1)S(1)} custom-call(s32[1]{0:T(128)S(6)} %copy.12.start_hbm, s32[1]{0:T(128)S(6)} %copy.13.length_hbm, bf16[512,1024]{1,0:T(8,128)(2,1)} %frames.1, bf16[32,1024]{1,0:T(8,128)(2,1)} %bitcast.5, bf16[16,1024]{1,0:T(8,128)(2,1)} %bitcast.6, f32[1,1024]{1,0:T(1,128)} %bitcast.7, f32[31,1024]{1,0:T(8,128)} %taps_hbm.1, ...), custom_call_target="tpu_custom_call" | custom-call | tf_op jit(solution)/shard_map/conformer_conv/pallas_call | solution.py:417
  44.4 1.0 %copy.11 = bf16[512,1024]{1,0:T(8,128)(2,1)} copy(bf16[512,1024]{1,0:T(8,128)(2,1)S(1)} %conformer_conv.1) | data formatting | bytes 2097152

commit v4 on v3

v4 whole, which is shorter than its diff:
```python
import jax
import jax.numpy as jnp
from jax import lax
from jax.experimental import pallas as pl
from jax.experimental.pallas import tpu as pltpu
from jax.sharding import PartitionSpec as P

MESH = pl.DeviceIdType.MESH
BF16, F32 = jnp.bfloat16, jnp.float32
NT = (((1,), (1,)), ((), ()))

ROWS = 512
HALO = 16
SPAN = ROWS + 2 * HALO
D = 1024
TAPS = 31
OUT = 16
NX, NY, NZ = 4, 4, 8
LB = 512
VMEM_BYTES = 58 * 1024 * 1024
CONV_ROWS = 256


def remote(src, dst, send_sem, recv_sem, device):
    return pltpu.make_async_remote_copy(
        src_ref=src, dst_ref=dst, send_sem=send_sem, recv_sem=recv_sem, device_id=device, device_id_type=MESH
    )


def kernel(
    start_hbm, length_hbm, frames, w_in, w_out, gain_hbm, taps_hbm, scale_hbm, shift_hbm, out,
    fbuf, normed, wout, W, WO, G, conv_in, act, acc, gain, raw_taps, raw_scale, raw_shift, params, start, length,
    local_sem, halo_s, halo_r, zin_s, zin_r, yin_s, yin_r, din_s, din_r,
    x_s, x_r, xf_s, xf_r, zo_s, zo_r, xo_s, xo_r, yo_s, yo_r, do_s, do_r,
    yb_s, yb_r, zb_s, zb_r, db_s, db_r,
):
    var, tm = lax.axis_index("var"), lax.axis_index("tm")
    y_hi, x = var // NX, lax.rem(var, NX)
    z, y_lo, core = tm // (2 * NY), lax.rem(tm // 2, NY), lax.rem(tm, 2)
    y = y_hi * NY + y_lo

    def at_y(step):
        there = lax.rem(y + step, 2 * NY)
        return ((there // NY) * NX + x, z * 2 * NY + lax.rem(there, NY) * 2 + core)

    def at_z(step):
        return (var, lax.rem(z + step, NZ) * 2 * NY + y_lo * 2 + core)

    def at_x(step):
        return (y_hi * NX + lax.rem(x + step, NX), tm)

    partner = (var, z * 2 * NY + y_lo * 2 + (1 - core))
    up = jnp.where((core == 1) & (y_lo == NY - 1), 1 - y_hi, y_hi)
    down = jnp.where((core == 0) & (y_lo == 0), 1 - y_hi, y_hi)
    after = (up * NX + x, lax.rem(tm + 1, 2 * NY * NZ))
    before = (down * NX + x, lax.rem(tm + 2 * NY * NZ - 1, 2 * NY * NZ))

    barrier = pltpu.get_barrier_semaphore()
    friends = [at_z(k) for k in (2, 6, 1, 7)] + [at_y(2), at_y(6), at_y(1), at_y(7)]
    friends += [at_x(2), at_x(1), at_x(3), after, before, partner]
    for device in friends:
        pl.semaphore_signal(barrier, inc=1, device_id=device, device_id_type=MESH)

    fetch = [
        pltpu.make_async_copy(src, dst, local_sem.at[i])
        for i, (src, dst) in enumerate(
            (
                (w_out, wout),
                (frames, fbuf.at[pl.ds(HALO, ROWS)]),
                (taps_hbm, raw_taps),
                (scale_hbm, raw_scale),
                (shift_hbm, raw_shift),
                (gain_hbm, gain),
                (start_hbm, start),
                (length_hbm, length),
            )
        )
    ]
    for copy in fetch:
        copy.start()

    role = z // 4
    depth = lax.rem(z - x + NZ, NZ)
    is_source = lax.rem(depth, 4) == 0

    pieces = ((0, pl.ds(0, D // 2)), (0, pl.ds(D // 2, D // 2)), (1, pl.ds(0, D)))
    two_steps = (2, 6, 1, 7)

    def own_slot(i):
        c, lanes = pieces[i]
        return pltpu.make_async_copy(
            w_in.at[pl.ds(c * OUT, OUT), lanes], W.at[c, role, y_lo, core, :, lanes], local_sem.at[9 + i]
        )

    def zin(i, k):
        c, lanes = pieces[i]
        return remote(
            w_in.at[pl.ds(c * OUT, OUT), lanes], W.at[c, role, y_lo, core, :, lanes],
            zin_s.at[i, k], zin_r.at[i, role], at_z(k),
        )

    @pl.when(is_source)
    def _():
        for i in range(3):
            own_slot(i).start()

    pl.semaphore_wait(barrier, len(friends))

    @pl.when(is_source)
    def _():
        for i in (0, 1):
            for k in two_steps:
                zin(i, k).start()

    old = lax.broadcasted_iota(jnp.int32, (256, 256), 0)
    new = lax.broadcasted_iota(jnp.int32, (256, 256), 1)
    order = (old // 32 == (new // 16) % 8) & ((old // 16) % 2 == new // 128) & (old % 16 == new % 16)
    order = jnp.where(order, 1.0, 0.0)

    back = pl.ds(LB, D - LB)
    front = pl.ds(0, LB)

    fetch[0].wait()
    for b in range(4):
        lanes = pl.ds(b * 256, 256)
        wout[:, lanes] = jnp.dot(wout[:, lanes], order.astype(BF16), preferred_element_type=F32).astype(BF16)
    WO[z, y_lo, core, :, :LB] = wout[:, :LB]

    def zo(k):
        piece = WO.at[z, y_lo, core, :, back]
        return remote(piece, piece, zo_s.at[k], zo_r.at[role], at_z(k))

    @pl.when(is_source)
    def _():
        WO[z, y_lo, core, :, LB:] = wout[:, LB:]
        for k in two_steps:
            zo(k).start()
        for k in two_steps:
            zin(2, k).start()

    def yb(j):
        piece = WO.at[z, y_lo, core, :, front]
        return remote(piece, piece, yb_s.at[j], yb_r.at[j], at_y((0, 1, 7, 2)[j]))

    for j in (3, 1, 2):
        yb(j).start()

    fetch[1].wait()
    tail = remote(fbuf.at[pl.ds(ROWS, HALO)], fbuf.at[pl.ds(0, HALO)], halo_s.at[0], halo_r.at[0], after)
    head = remote(fbuf.at[pl.ds(HALO, HALO)], fbuf.at[pl.ds(HALO + ROWS, HALO)], halo_s.at[1], halo_r.at[1], before)
    tail.start()
    head.start()

    for copy in fetch[2:]:
        copy.wait()
    for b in range(4):
        lanes = pl.ds(b * 256, 256)
        for first, src in ((0, raw_taps), (32, raw_scale), (40, raw_shift)):
            params[pl.ds(first, src.shape[0]), lanes] = jnp.dot(
                src[:, lanes], order, precision=lax.Precision.HIGHEST, preferred_element_type=F32
            )

    def normalize(row, count, keep):
        values = fbuf[pl.ds(row, count)].astype(F32)
        average = jnp.mean(values, axis=1, keepdims=True)
        centred = values - average
        variance = jnp.mean(centred * centred, axis=1, keepdims=True)
        result = centred * lax.rsqrt(variance + 1e-05) * gain[...]
        if keep is not None:
            result = jnp.where(keep, result, 0.0)
        normed[pl.ds(row, count)] = result.astype(BF16)

    for i in (0, 1):
        normalize(HALO + i * 128, 128, None)

    near = jnp.where((depth <= 2) | (depth >= 6), 0, 1)
    roles = (near, 1 - near)

    def line(j):
        return lax.rem(y_lo + (0, 3, 1, 2)[j], NY)

    def yin(i, r, j):
        c, lanes = pieces[i]
        piece = W.at[c, r, y_lo, core, :, lanes]
        device = {1: at_y(1), 2: at_y(7), 3: at_y(2 + 4 * r)}[j]
        return remote(piece, piece, yin_s.at[i, r, j], yin_r.at[i, r, j], device)

    def yin_arrival(i, r, j):
        c, lanes = pieces[i]
        piece = W.at[c, r, line(j), core, :, lanes]
        return remote(piece, piece, yin_s.at[i, r, j], yin_r.at[i, r, j], partner)

    def din(c, r, j):
        piece = W.at[c, r, line(j), core]
        return remote(piece, piece, din_s.at[c, r, j], din_r.at[c, r, j], partner)

    def din_arrival(c, r, j):
        piece = W.at[c, r, line(j), 1 - core]
        return remote(piece, piece, din_s.at[c, r, j], din_r.at[c, r, j], partner)

    def relay(r, piece, send_sem, recv_sem):
        @pl.when(depth == 2 + 4 * r)
        def _():
            remote(piece, piece, send_sem(3), recv_sem, at_z(1)).start()
            remote(piece, piece, send_sem(4), recv_sem, at_z(2)).start()

        @pl.when(depth == 6 - 4 * r)
        def _():
            remote(piece, piece, send_sem(5), recv_sem, at_z(7)).start()

    def pass_on(i):
        c, lanes = pieces[i]
        for r in roles:
            piece = W.at[c, r, y_lo, core, :, lanes]

            @pl.when(depth == 4 * r)
            def _():
                own_slot(i).wait()

            @pl.when(depth != 4 * r)
            def _(r=r, piece=piece):
                remote(piece, piece, zin_s.at[i, 0], zin_r.at[i, r], partner).wait_recv()

            relay(r, piece, lambda k: zin_s.at[i, k], zin_r.at[i, r])
            for j in (3, 1, 2):
                yin(i, r, j).start()
            if i:
                din(i - 1, r, 0).start()

    def xo(r, w):
        piece = WO.at[x + 4 * r, y_lo, core, :, back]
        return remote(piece, piece, xo_s.at[r, w], xo_r.at[r, w], at_x((2, 1, 3)[w]))

    def pass_back():
        for r in roles:
            piece = WO.at[x + 4 * r, y_lo, core, :, back]

            @pl.when(depth != 4 * r)
            def _(r=r, piece=piece):
                remote(piece, piece, zo_s.at[0], zo_r.at[r], partner).wait_recv()

            relay(r, piece, lambda k: zo_s.at[k], zo_r.at[r])
            for w in range(3):
                xo(r, w).start()

    pass_on(0)
    pass_on(1)
    pass_back()
    normalize(HALO + 256, 128, None)
    pass_on(2)

    for j in (1, 2, 3):
        piece = WO.at[z, line(j), core, :, front]
        remote(piece, piece, yb_s.at[j], yb_r.at[j], partner).wait_recv()

    def zb_piece(k, base):
        rows = {4: pl.ds(0, 2), 0: pl.ds(2, 2)}.get(k, pl.ds(0, NY))
        return WO.at[lax.rem(base + NZ - (k or 4), NZ), rows, core, :, front]

    def zb(k):
        step = {3: 1, 5: 7, 4: 2, 0: 6}.get(k, k)
        piece = zb_piece(k, lax.rem(z + step, NZ))
        return remote(piece, piece, zb_s.at[k], zb_r.at[k], at_z(step))

    def zb_arrival(k):
        piece = zb_piece(k, z)
        return remote(piece, piece, zb_s.at[k], zb_r.at[k], partner)

    for k in (1, 7, 2, 6):
        zb(k).start()

    normalize(HALO + 384, 128, None)
    tail.wait_recv()
    head.wait_recv()
    normalize(0, HALO, tm > 0)
    normalize(HALO + ROWS, HALO, tm < 2 * NY * NZ - 1)

    def lift(c):
        columns = jnp.concatenate([W[c, 0].reshape(128, D), W[c, 1].reshape(128, D)], axis=0)
        lifted = lax.dot_general(normed[...], columns, NT, preferred_element_type=F32)
        G[x, c] = (lifted[:, :128] * jax.nn.sigmoid(lifted[:, 128:])).astype(BF16)

    parts = (pl.ds(0, SPAN // 2), pl.ds(SPAN // 2, SPAN // 2))

    def x_copy(c, way, p):
        piece = G.at[x, c, parts[p]]
        return remote(piece, piece, x_s.at[c, way, p], x_r.at[c, way, p], at_x((1, 3)[way]))

    def x_arrival(c, way, p):
        piece = G.at[lax.rem(x + (3, 1)[way], NX), c, parts[p]]
        return remote(piece, piece, x_s.at[c, way, p], x_r.at[c, way, p], partner)

    def x_forward(c, p):
        piece = G.at[lax.rem(x + (3, 1)[p], NX), c, parts[p]]
        return remote(piece, piece, xf_s.at[c, p], xf_r.at[c, p], at_x((1, 3)[p]))

    def x_far(c, p):
        piece = G.at[lax.rem(x + 2, NX), c, parts[p]]
        return remote(piece, piece, xf_s.at[c, p], xf_r.at[c, p], partner)

    row0 = tm * ROWS
    span_low, span_high = start[0], start[0] + length[0]

    def occluded(begin, count):
        position = begin + lax.broadcasted_iota(jnp.int32, (count, 1), 0)
        return (position >= span_low) & (position < span_high)

    def convolve(step, c):
        owner = lax.rem(x + step, NX)
        lanes = pl.ds(pl.multiple_of(owner * 256 + c * 128, 128), 128)
        conv_in[...] = jnp.where(occluded(row0 - HALO, SPAN), 0.0, G[owner, c].astype(F32))

        @pl.loop(0, ROWS // CONV_ROWS)
        def _(i):
            row = pl.multiple_of(i * CONV_ROWS, CONV_ROWS)
            total = None
            for j in range(TAPS):
                term = conv_in[pl.ds(row + j + 1, CONV_ROWS)] * params[pl.ds(j, 1), lanes]
                total = term if total is None else total + term
            value = total * params[pl.ds(32, 1), lanes] + params[pl.ds(40, 1), lanes]
            act[owner, pl.ds(row, CONV_ROWS), pl.ds(c * 128, 128)] = (value * jax.nn.sigmoid(value)).astype(BF16)

    def product(step, n, first=0, count=256):
        owner = lax.rem(x + step, NX)
        depths = pl.ds(pl.multiple_of(owner * 256 + first, 128), count)
        columns = WO[2 * n : 2 * n + 2, :, :, :, depths].reshape(256, count)
        return lax.dot_general(act[owner, :, first : first + count], columns, NT, preferred_element_type=F32)

    def gather_core(c):
        for j in (1, 2, 3):
            for r in roles:
                for i in (0, 1) if c == 0 else (2,):
                    yin_arrival(i, r, j).wait_recv()
                din(c, r, j).start()

    def lift_and_send(c):
        for j in range(4):
            for r in (0, 1):
                din_arrival(c, r, j).wait_recv()
        lift(c)
        for p in (0, 1):
            for way in (0, 1):
                x_copy(c, way, p ^ way).start()

    gather_core(0)
    lift_and_send(0)

    for w in range(3):
        for r in (0, 1):
            piece = WO.at[lax.rem(x + (2, 3, 1)[w], NX) + 4 * r, y_lo, core, :, back]
            remote(piece, piece, xo_s.at[r, w], xo_r.at[r, w], partner).wait_recv()

    full = WO.at[:, y_lo, core, :, back]
    low, high = WO.at[pl.ds(0, NZ // 2), y_lo, core, :, back], WO.at[pl.ds(NZ // 2, NZ // 2), y_lo, core, :, back]
    yo = [
        remote(low, low, yo_s.at[2], yo_r.at[2], at_y(2)),
        remote(high, high, yo_s.at[3], yo_r.at[3], at_y(6)),
        remote(full, full, yo_s.at[0], yo_r.at[0], at_y(1)),
        remote(full, full, yo_s.at[1], yo_r.at[1], at_y(7)),
    ]
    for copy in yo:
        copy.start()

    def do(j):
        piece = WO.at[:, line(j), core, :, back]
        return remote(piece, piece, do_s.at[j], do_r.at[j], partner)

    do(0).start()

    gather_core(1)
    lift_and_send(1)

    for k in (1, 7, 2, 6):
        zb_arrival(k).wait_recv()
    for k in (4, 0, 3, 5):
        zb(k).start()

    for p in (0, 1):
        x_arrival(0, p, p).wait_recv()
        x_forward(0, p).start()
    convolve(0, 0)
    convolve(0, 1)
    for p in (0, 1):
        x_arrival(0, p, 1 - p).wait_recv()
    convolve(1, 0)
    convolve(3, 0)
    for p in (0, 1):
        x_arrival(1, p, p).wait_recv()
        x_forward(1, p).start()

    for j in (1, 2):
        piece = WO.at[:, line(j), core, :, back]
        remote(piece, piece, yo_s.at[0], yo_r.at[j - 1], partner).wait_recv()
        do(j).start()
    for p in (0, 1):
        x_arrival(1, p, 1 - p).wait_recv()
    convolve(1, 1)
    for h in (0, 1):
        piece = WO.at[pl.ds(h * 4, 4), line(3), core, :, back]
        remote(piece, piece, yo_s.at[0], yo_r.at[2 + h], partner).wait_recv()
    do(3).start()
    for k in (3, 5, 4, 0):
        zb_arrival(k).wait_recv()
    mine = WO.at[:, :, core, :, front]
    db = remote(mine, mine, db_s.at[0], db_r.at[0], partner)
    db.start()
    convolve(3, 1)

    for p in (0, 1):
        x_far(0, p).wait_recv()
    convolve(2, 0)

    for j in range(4):
        piece = WO.at[:, line(j), 1 - core, :, back]
        remote(piece, piece, do_s.at[j], do_r.at[j], partner).wait_recv()
    theirs = WO.at[:, :, 1 - core, :, front]
    remote(theirs, theirs, db_s.at[0], db_r.at[0], partner).wait_recv()

    for n in range(4):
        acc[n] = product(0, n) + product(1, n) + product(3, n) + product(2, n, 0, 128)

    for p in (0, 1):
        x_far(1, p).wait_recv()
    convolve(2, 1)

    for n in range(4):
        lanes = pl.ds(n * 256, 256)
        masked = jnp.where(occluded(row0, ROWS), 0.0, fbuf[pl.ds(HALO, ROWS), lanes].astype(F32))
        out[:, lanes] = (masked + (acc[n] + product(2, n, 128, 128))).astype(BF16)

    @pl.when(is_source)
    def _():
        for k in two_steps:
            for i in range(3):
                zin(i, k).wait_send()
            zo(k).wait_send()

    @pl.when(lax.rem(depth, 4) == 2)
    def _():
        back_piece = WO.at[z, y_lo, core, :, back]
        for k in (3, 4, 5):
            for i, (c, lanes) in enumerate(pieces):
                piece = W.at[c, role, y_lo, core, :, lanes]
                remote(piece, piece, zin_s.at[i, k], zin_r.at[i, 0], partner).wait_send()
            remote(back_piece, back_piece, zo_s.at[k], zo_r.at[0], partner).wait_send()

    tail.wait_send()
    head.wait_send()
    for c in (0, 1):
        for r in (0, 1):
            for j in range(4):
                din(c, r, j).wait_send()
        for p in (0, 1):
            for way in (0, 1):
                x_copy(c, way, p).wait_send()
            x_forward(c, p).wait_send()
    for r in (0, 1):
        for j in (1, 2, 3):
            for i in range(3):
                yin(i, r, j).wait_send()
        for w in range(3):
            xo(r, w).wait_send()
    for j in (1, 2, 3):
        yb(j).wait_send()
    for k in range(NZ):
        zb(k).wait_send()
    for copy in yo:
        copy.wait_send()
    for j in range(4):
        do(j).wait_send()
    db.wait_send()


def module(frames, span_start, span_length, ln_gain, w_in, taps, bn_scale, bn_shift, w_out):
    hbm = pl.BlockSpec(memory_space=pl.ANY)
    dma = pltpu.SemaphoreType.DMA
    return pl.pallas_call(
        kernel,
        name="conformer_conv",
        out_shape=pltpu.VMEM((ROWS, D), BF16),
        in_specs=[hbm] * 9,
        out_specs=pl.BlockSpec(memory_space=pltpu.VMEM),
        scratch_shapes=[
            pltpu.VMEM((SPAN, D), BF16),
            pltpu.VMEM((SPAN, D), BF16),
            pltpu.VMEM((OUT, D), BF16),
            pltpu.VMEM((2, 2, NY, 2, OUT, D), BF16),
            pltpu.VMEM((NZ, NY, 2, OUT, D), BF16),
            pltpu.VMEM((NX, 2, SPAN, 128), BF16),
            pltpu.VMEM((SPAN, 128), F32),
            pltpu.VMEM((NX, ROWS, 256), BF16),
            pltpu.VMEM((4, ROWS, 256), F32),
            pltpu.VMEM((1, D), F32),
            pltpu.VMEM((TAPS, D), F32),
            pltpu.VMEM((1, D), F32),
            pltpu.VMEM((1, D), F32),
            pltpu.VMEM((48, D), F32),
            pltpu.SMEM((1,), jnp.int32),
            pltpu.SMEM((1,), jnp.int32),
            dma((12,)),
            dma((2,)), dma((2,)),
            dma((3, NZ)), dma((3, 2)),
            dma((3, 2, 4)), dma((3, 2, 4)),
            dma((2, 2, 4)), dma((2, 2, 4)),
            dma((2, 2, 2)), dma((2, 2, 2)),
            dma((2, 2)), dma((2, 2)),
            dma((NZ,)), dma((2,)),
            dma((2, 3)), dma((2, 3)),
            dma((4,)), dma((4,)),
            dma((4,)), dma((4,)),
            dma((4,)), dma((4,)),
            dma((NZ,)), dma((NZ,)),
            dma((1,)), dma((1,)),
        ],
        compiler_params=pltpu.CompilerParams(
            collective_id=0, has_side_effects=True, vmem_limit_bytes=VMEM_BYTES
        ),
    )(
        span_start, span_length, frames, w_in.T, w_out.T, ln_gain.reshape(1, D), taps,
        bn_scale.reshape(1, D), bn_shift.reshape(1, D),
    )


def solution(mesh):
    return jax.shard_map(
        module,
        mesh=mesh,
        in_specs=(P("tm", None), P("var"), P("var"), P(), P(None, "tm"), P(), P(), P(), P(None, "tm")),
        out_specs=P(("var", "tm"), None),
        check_vma=False,
    )
```

time: 45.5 us -> 45.1 us (level)
  no operation moved by 1% of the time
where the time goes in v4:
time: 45.1 us; the launch traced here: 45 us
  Pallas kernels  42.7 us (95%)
  between operations  1.3 us (3%)
  local copies, waits for them, and re-layouts  0.97 us (2%)
    pallas_call x1, Pallas kernels, module(): pl.pallas_call(kernel, name='conformer_conv', out_shape=pltpu.VMEM((ROWS,...  42.7 us
    unnamed x1, local copies, waits for them, and re-layouts  0.97 us

profile of v4, /device:TPU:1, one launch (start us, length us, event | category | flops | bytes accessed | tf_op | source)
XLA Modules:
  0.0 45.0 jit_solution(5440367941460611020)
XLA Ops:
  1.3 42.7 %conformer_conv.1 = bf16[512,1024]{1,0:T(8,128)(2,1)S(1)} custom-call(s32[1]{0:T(128)S(6)} %copy.12.start_hbm, s32[1]{0:T(128)S(6)} %copy.13.length_hbm, bf16[512,1024]{1,0:T(8,128)(2,1)} %frames.1, bf16[32,1024]{1,0:T(8,128)(2,1)} %bitcast.5, bf16[16,1024]{1,0:T(8,128)(2,1)} %bitcast.6, f32[1,1024]{1,0:T(1,128)} %bitcast.7, f32[31,1024]{1,0:T(8,128)} %taps_hbm.1, ...), custom_call_target="tpu_custom_call" | custom-call | tf_op jit(solution)/shard_map/conformer_conv/pallas_call | solution.py:477
  44.0 1.0 %copy.11 = bf16[512,1024]{1,0:T(8,128)(2,1)} copy(bf16[512,1024]{1,0:T(8,128)(2,1)S(1)} %conformer_conv.1) | data formatting | bytes 2097152

commit v5 on v3

--- a/solution.py
+++ b/solution.py
@@ -17,9 +17,13 @@
 VAL = 32
 OUT = 16
 NX, NY, NZ = 4, 4, 8
-LB = 384
+LB = 512
 VMEM_BYTES = 58 * 1024 * 1024
-CONV_ROWS = 128
+CONV_ROWS = 256
+
+
+def sigmoid(values):
+    return 0.5 + 0.5 * jnp.tanh(0.5 * values)
 
 
 def remote(src, dst, send_sem, recv_sem, device):
@@ -231,7 +235,7 @@
     def lift(c):
         columns = jnp.concatenate([W[c, 0].reshape(128, D), W[c, 1].reshape(128, D)], axis=0)
         lifted = lax.dot_general(normed[...], columns, NT, preferred_element_type=F32)
-        G[x, c] = (lifted[:, :128] * jax.nn.sigmoid(lifted[:, 128:])).astype(BF16)
+        G[x, c] = (lifted[:, :128] * sigmoid(lifted[:, 128:])).astype(BF16)
 
     parts = (pl.ds(0, SPAN // 2), pl.ds(SPAN // 2, SPAN // 2))
 
@@ -310,13 +314,13 @@
                 term = conv_in[pl.ds(row + j + 1, CONV_ROWS)] * params[pl.ds(j, 1), lanes]
                 total = term if total is None else total + term
             value = total * params[pl.ds(32, 1), lanes] + params[pl.ds(40, 1), lanes]
-            act[owner, pl.ds(row, CONV_ROWS), pl.ds(c * 128, 128)] = (value * jax.nn.sigmoid(value)).astype(BF16)
-
-    def product(step, n):
+            act[owner, pl.ds(row, CONV_ROWS), pl.ds(c * 128, 128)] = (value * sigmoid(value)).astype(BF16)
+
+    def product(step, n, first=0, count=256):
         owner = lax.rem(x + step, NX)
-        depths = pl.ds(pl.multiple_of(owner * 256, 256), 256)
-        columns = WO[2 * n : 2 * n + 2, :, :, :, depths].reshape(256, 256)
-        return lax.dot_general(act[owner], columns, NT, preferred_element_type=F32)
+        depths = pl.ds(pl.multiple_of(owner * 256 + first, 128), count)
+        columns = WO[2 * n : 2 * n + 2, :, :, :, depths].reshape(256, count)
+        return lax.dot_general(act[owner, :, first : first + count], columns, NT, preferred_element_type=F32)
 
     convolve(0, 0)
     convolve(0, 1)
@@ -364,10 +368,7 @@
     remote(theirs, theirs, db_s.at[0], db_r.at[0], partner).wait_recv()
 
     for n in range(4):
-        acc[n] = product(0, n)
-    for step in (1, 3):
-        for n in range(4):
-            acc[n] += product(step, n)
+        acc[n] = product(0, n) + product(1, n) + product(3, n) + product(2, n, 0, 128)
 
     for p in (0, 1):
         x_far(1, p).wait_recv()
@@ -376,7 +377,7 @@
     for n in range(4):
         lanes = pl.ds(n * 256, 256)
         masked = jnp.where(occluded(row0, ROWS), 0.0, fbuf[pl.ds(HALO, ROWS), lanes].astype(F32))
-        out[:, lanes] = (masked + (acc[n] + product(2, n))).astype(BF16)
+        out[:, lanes] = (masked + (acc[n] + product(2, n, 128, 128))).astype(BF16)
 
     @pl.when(is_source)
     def _():

time: 45.5 us -> 45.4 us (level)
  no operation moved by 1% of the time
where the time goes in v5:
time: 45.4 us; the launch traced here: 45.3 us
  Pallas kernels  43 us (95%)
  between operations  1.3 us (3%)
  local copies, waits for them, and re-layouts  0.97 us (2%)
    pallas_call x1, Pallas kernels, module(): pl.pallas_call(kernel, name='conformer_conv', out_shape=pltpu.VMEM((ROWS,...  43 us
    unnamed x1, local copies, waits for them, and re-layouts  0.97 us

profile of v5, /device:TPU:1, one launch (start us, length us, event | category | flops | bytes accessed | tf_op | source)
XLA Modules:
  0.0 45.3 jit_solution(13578278516105642984)
XLA Ops:
  1.3 43.0 %conformer_conv.1 = bf16[512,1024]{1,0:T(8,128)(2,1)S(1)} custom-call(s32[1]{0:T(128)S(6)} %copy.12.start_hbm, s32[1]{0:T(128)S(6)} %copy.13.length_hbm, bf16[512,1024]{1,0:T(8,128)(2,1)} %frames.1, bf16[32,1024]{1,0:T(8,128)(2,1)} %bitcast.5, bf16[16,1024]{1,0:T(8,128)(2,1)} %bitcast.6, f32[1,1024]{1,0:T(1,128)} %bitcast.7, f32[31,1024]{1,0:T(8,128)} %taps_hbm.1, ...), custom_call_target="tpu_custom_call" | custom-call | tf_op jit(solution)/shard_map/conformer_conv/pallas_call | solution.py:418
  44.3 1.0 %copy.11 = bf16[512,1024]{1,0:T(8,128)(2,1)} copy(bf16[512,1024]{1,0:T(8,128)(2,1)S(1)} %conformer_conv.1) | data formatting | bytes 2097152
